TPU v7x, 32 devices: a whole 2x2x4 slice. The times are simulated.
32 devices in a mesh: groups: 2 (over y), replica: 8 (over z, x), tensor: 2 (over core).
Axes of the slice: x: 2, y: 2, z: 4, core: 2. Of those that a mesh axis runs over, the one named last changes fastest.
Arguments:
- tokens: bfloat16 [4096, 8192], P(('groups', 'replica'), 'tensor'), parts along dimension 0, may hold values from -6 to 6
- key_weight: bfloat16 [8192, 512], P('replica', 'tensor'), may hold values from -0.0625 to 0.0625
- down_proj: bfloat16 [256, 16, 8192], P(('groups', 'replica'), None, 'tensor'), parts along dimension 0, may hold values from -0.0625 to 0.0625
- up_proj: bfloat16 [256, 16, 512], P(('groups', 'replica'), None, 'tensor'), parts along dimension 0, may hold values from -0.75 to 0.75
- tenant_of_row: int32 [4096], P(('groups', 'replica')), parts along dimension 0, may hold values from 0 to 127, as said below
- page_of_tenant: int32 [256], P('groups'), parts along dimension 0, may hold values from 0 to 127, as said below
Outputs:
- adapted_key_output: bfloat16 [4096, 512], P(('groups', 'replica'), 'tensor'), parts along dimension 0
There are 2 independent parts, one for each index of `groups`. A program takes and returns all parts, laid end to end along the dimension named above; an argument that names none is the same for every part. Nothing has to cross between parts.
Inputs may be any that keep to these rules, and one draw needn't show every extreme that they name: Tenant t's adapter is page page_of_tenant[t]; page p is stored on replica p // 16. Every page belongs to exactly one tenant. `tenant_of_row`: within the rows of one replica (aligned blocks of 256 rows) no tenant appears more than 2 times, and this bound is reached.
All inputs are finite; a program needn't handle non-finite values.
Results may differ from a plain program's by a relative error of at most 0.001.
Values may be sent and summed in bfloat16 or wider, within the bound.
A program may use at most 64 MiB of HBM per device.

v0:
```python
import jax
import jax.numpy as jnp
from jax import lax
from jax.sharding import PartitionSpec as P

MOST = 2


adapter_scale = 2.0


def per_device(tokens, key_weight, down_proj, up_proj, tenant_of_row, page_of_tenant):
    row_count = tokens.shape[0]
    ten_dev = down_proj.shape[0]
    replicas = lax.axis_size("replica")
    slot_count = replicas * ten_dev * MOST
    page_row = page_of_tenant[tenant_of_row]
    owner_rep = page_row // ten_dev
    local_page = page_row % ten_dev
    same_tenant = tenant_of_row[:, None] == tenant_of_row[None, :]
    row_index = jnp.arange(row_count, dtype=jnp.int32)
    earlier = row_index[None, :] < row_index[:, None]
    row_rank = jnp.sum((same_tenant & earlier).astype(jnp.int32), axis=1)
    row_slot = (owner_rep * ten_dev + local_page) * MOST + row_rank
    slot_source = jnp.full((slot_count,), row_count, jnp.int32).at[row_slot].set(row_index)
    gathered = lax.all_gather(tokens, "tensor", axis=1, tiled=True)
    base_total_sum = jnp.dot(
        gathered,
        lax.all_gather(key_weight, "replica", axis=0, tiled=True),
        preferred_element_type=jnp.float32,
    )
    padded = jnp.concatenate([tokens, jnp.zeros((1, tokens.shape[1]), tokens.dtype)], axis=0)
    packed = jnp.take(padded, slot_source, axis=0).reshape(replicas, ten_dev, MOST, tokens.shape[1])
    received_parts = lax.all_to_all(packed, "replica", split_axis=0, concat_axis=0, tiled=True)
    partial_value = jnp.einsum(
        "sjmd,jrd->sjmr", received_parts, down_proj, preferred_element_type=jnp.float32
    )
    shrink = lax.psum(partial_value, "tensor")
    adapter_delta_rows = jnp.einsum(
        "sjmr,jrc->sjmc", shrink, up_proj.astype(jnp.float32), precision=lax.Precision.HIGHEST
    )
    adapter_delta_rows = adapter_delta_rows.reshape(replicas, ten_dev * MOST, up_proj.shape[2])
    returned = lax.all_to_all(
        adapter_delta_rows, "replica", split_axis=0, concat_axis=0, tiled=True
    )
    per_row_delta = jnp.take(returned.reshape(slot_count, up_proj.shape[2]), row_slot, axis=0)
    return (base_total_sum + adapter_scale * per_row_delta).astype(jnp.bfloat16)


def solution(mesh):
    return jax.shard_map(
        per_device,
        mesh=mesh,
        in_specs=(
            P(("groups", "replica"), "tensor"),
            P("replica", "tensor"),
            P(("groups", "replica"), None, "tensor"),
            P(("groups", "replica"), None, "tensor"),
            P(("groups", "replica")),
            P("groups"),
        ),
        out_specs=P(("groups", "replica"), "tensor"),
        check_vma=False,
    )
```

profile of v0, /device:TPU:0, one launch (start us, length us, event | category | flops | bytes accessed | tf_op | source)
XLA Modules:
  0.0 161.1 jit_solution(11362772908153280995)
XLA Ops:
  6.5 0.0 copy-start
  6.5 0.0 all-gather.3.cloned.1.call-start
  6.5 0.7 all-gather.3.cloned.1.call-update
  7.3 0.0 all-gather.5.cloned.1.call-start
  7.3 0.7 all-gather.5.cloned.1.call-update
  8.0 0.0 copy-start.3
  8.0 0.0 copy-start.1
  8.0 3.2 %concatenate.3 = bf16[257,4096]{1,0:T(8,128)(2,1)} pad(bf16[256,4096]{1,0:T(8,128)(2,1)} %param.6, bf16[]{:T(256)} %constant.67.clone.1), padding=0_1x0_0 | pad | bytes 4202498 | tf_op jit(solution)/shard_map/concatenate | solution.py:32
  11.3 0.0 copy-done.3
  11.3 0.0 copy-done.1
  11.3 1.9 %gather_fusion = s32[256]{0:T(256)S(1)} fusion(s32[128]{0:T(128)S(1)} %copy-done.1, s32[1024]{0:T(1024)S(1)} %pad_clamp_fusion.2), kind=kCustom, calls=%fused_computation | custom fusion | bytes 3072 | tf_op jit(solution)/shard_map/gather | solution.py:17
  13.2 0.2 convert_reduce_fusion
  13.4 1.4 scatter_custom_fusion
  14.8 7.1 %gather_fusion.1 = bf16[256,4096]{1,0:T(8,128)(2,1)} fusion(bf16[257,4096]{1,0:T(8,128)(2,1)} %concatenate.3, s32[1024]{0:T(1024)S(1)} %pad_clamp_fusion.1), kind=kCustom, calls=%fused_computation.1 | custom fusion | bytes 4195328 | tf_op jit(solution)/shard_map/jit(_take)/gather | solution.py:33
  21.9 4.6 %gather.18 = bf16[8,16,2,4096]{3,2,1,0:T(2,128)(2,1)} reshape(bf16[256,4096]{1,0:T(8,128)(2,1)} %gather_fusion.1) | data formatting | bytes 4194304 | tf_op jit(solution)/shard_map/jit(_take)/gather | solution.py:33
  26.5 0.2 broadcast_in_dim.35
  26.7 3.7 %broadcast_select_fusion = bf16[8,16,2,4096]{3,2,1,0:T(2,128)(2,1)S(1)} fusion(bf16[8,16,2,4096]{3,2,1,0:T(2,128)(2,1)} %gather.18, pred[8,16,2]{2,1,0:T(8,128)(4,1)S(1)} %broadcast_in_dim.35), kind=kLoop, calls=%fused_computation.4 | loop fusion | flops 1048576 | bytes 4194560 | tf_op jit(solution)/shard_map/jit(_take)/select_n | solution.py:33
  30.4 98.1 %all_to_all.10 = bf16[8,16,2,4096]{3,2,1,0:T(2,128)(2,1)S(1)} all-to-all(bf16[8,16,2,4096]{3,2,1,0:T(2,128)(2,1)S(1)} %broadcast_select_fusion), channel_id=1, replica_groups=mesh['groups'=2,'replica'=8,'tensor'=2] {'replica'}, dimensions={0} | all-to-all | bytes 4194304 | tf_op jit(solution)/shard_map/all_to_all | solution.py:34
  128.5 0.0 copy-done
  128.5 0.0 copy-start.2
  128.5 1.5 fusion.4
  130.0 3.7 %psum.7 = f32[8,16,2,16]{3,0,2,1:T(8,128)S(1)} all-reduce(f32[8,16,2,16]{3,0,2,1:T(8,128)S(1)} %fusion.4), channel_id=1, replica_groups=mesh['groups'=2,'replica'=8,'tensor'=2] {'tensor'}, use_global_device_ids=true, to_apply=%region_2.3 | all-reduce | flops 4096 | bytes 32768 | tf_op jit(solution)/shard_map/psum | solution.py:38
  133.7 0.0 copy-done.2
  133.7 0.2 fusion.10
  134.0 0.8 copy.17
  134.8 3.4 %all-to-all-start.1 = ((f32[8,32,256]{2,1,0:T(8,128)}), f32[8,32,256]{2,1,0:T(8,128)S(1)}, u32[]{:S(2)}, u32[]{:S(2)}) async-start(f32[8,32,256]{2,1,0:T(8,128)} %copy.17), calls=%async_computation.1 | async-start | bytes 524288 | tf_op jit(solution)/shard_map/all_to_all | solution.py:43
  138.2 9.6 %all-to-all-done.1 = f32[8,32,256]{2,1,0:T(8,128)S(1)} async-done(((f32[8,32,256]{2,1,0:T(8,128)}), f32[8,32,256]{2,1,0:T(8,128)S(1)}, u32[]{:S(2)}, u32[]{:S(2)}) %all-to-all-start.1) | async-done | bytes 262176 | tf_op jit(solution)/shard_map/all_to_all | solution.py:43
  147.8 1.0 gather_fusion.2
  148.8 0.0 all-gather.3.cloned.1.call-done
  148.8 0.0 all-gather.5.cloned.1.call-done
  148.9 5.4 %fusion.3 = bf16[256,256]{1,0:T(8,128)(2,1)} fusion(bf16[256,8192]{1,0:T(8,128)(2,1)} %all-gather.3.cloned.1.call-done, bf16[8192,256]{1,0:T(8,128)(2,1)} %all-gather.5.cloned.1.call-done, f32[256,256]{1,0:T(8,128)S(1)} %gather_fusion.2, pred[256]{0:T(512)(128)(4,1)S(1)} %compare_and_fusion.1), kind=kOutput, calls=%fused_computation.9 | convolution fusion | flops 1074003968 | bytes 8782080 | tf_op jit(solution)/shard_map/dot_general | solution.py:27
  (9 shorter events, 0.1 us)
Async XLA Ops:
  6.5 121.9 %copy-start = (bf16[16,16,4096]{2,1,0:T(8,128)(2,1)S(1)}, bf16[16,16,4096]{2,1,0:T(8,128)(2,1)}, u32[]{:S(2)}) copy-start(bf16[16,16,4096]{2,1,0:T(8,128)(2,1)} %param.8) | copy-start | bytes 6291460
  6.5 142.3 %all-gather.3.cloned.1.call-start = ((), (), s32[]{:S(2)}) async-start(), calls=%async_computation.2 | async-start | bytes 6291456 | tf_op jit(solution)/shard_map/all_gather | solution.py:26
  7.3 141.6 %all-gather.5.cloned.1.call-start = ((), (), s32[]{:S(2)}) async-start(), calls=%async_computation.3 | async-start | bytes 4718592 | tf_op jit(solution)/shard_map/all_gather | solution.py:29
  8.0 3.3 %copy-start.3 = (s32[256]{0:T(256)S(1)}, s32[256]{0:T(256)}, u32[]{:S(2)}) copy-start(s32[256]{0:T(256)} %param.10) | copy-start | bytes 3076
  8.0 3.3 %copy-start.1 = (s32[128]{0:T(128)S(1)}, s32[128]{0:T(128)}, u32[]{:S(2)}) copy-start(s32[128]{0:T(128)} %param.11) | copy-start | bytes 1540
  128.5 5.2 %copy-start.2 = (bf16[16,16,256]{2,1,0:T(8,128)(2,1)S(1)}, bf16[16,16,256]{2,1,0:T(8,128)(2,1)}, u32[]{:S(2)}) copy-start(bf16[16,16,256]{2,1,0:T(8,128)(2,1)} %param.9) | copy-start | bytes 393220
  134.8 13.1 %all-to-all-start.1 = ((f32[8,32,256]{2,1,0:T(8,128)}), f32[8,32,256]{2,1,0:T(8,128)S(1)}, u32[]{:S(2)}, u32[]{:S(2)}) async-start(f32[8,32,256]{2,1,0:T(8,128)} %copy.17), calls=%async_computation.1 | async-start | bytes 524288 | tf_op jit(solution)/shard_map/all_to_all | solution.py:43
Sparse Core Ops, SparseCore 0:
  8.9 16.3 all-gather.2
  27.4 109.0 all-gather.4
where the time goes:
time: 162 us; the launch traced here: 161 us
  blocking collectives  102 us (63%)
  local copies, waits for them, and re-layouts  20.1 us (12%)
  between operations  13.5 us (8%)
  waiting for transfers between devices  11.1 us (7%)
  matrix products  7.12 us (4%)
  other arithmetic  3.95 us (2%)
  starting transfers between devices  3.45 us (2%)
    all_to_all x1, blocking collectives, per_device(): lax.all_to_all(packed, 'replica', split_axis=0, concat_axis=0, tiled=True)  98.1 us
    gather x2, local copies, waits for them, and re-layouts, per_device(): jnp.take(padded, slot_source, axis=0)  11.7 us
    all_to_all x1, waiting for transfers between devices, per_device(): lax.all_to_all(adapter_delta_rows, 'replica', split_axis=0, concat_axis=0...  9.61 us
    dot_general x1, matrix products, per_device(): jnp.dot(gathered, lax.all_gather(key_weight, 'replica', axis=0, tiled=Tru...  5.38 us
    psum x1, blocking collectives, per_device(): shrink = lax.psum(partial_value, 'tensor')  3.74 us
    select_n x2, other arithmetic, per_device(): jnp.take(padded, slot_source, axis=0)  3.7 us
    all_to_all x1, starting transfers between devices, per_device(): lax.all_to_all(adapter_delta_rows, 'replica', split_axis=0, concat_axis=0...  3.41 us
    concatenate x1, local copies, waits for them, and re-layouts, per_device(): jnp.concatenate([tokens, jnp.zeros((1, tokens.shape[1]), tokens.dtype)],...  3.25 us
  transfers between devices with their start and end apart: 3, of which 1 were waited for; matrix products, arithmetic and copies ran while one was open for 16% of the time, Pallas kernels for 0%

commit v1 on v0

--- a/solution.py
+++ b/solution.py
@@ -1,15 +1,370 @@
+import functools
+
 import jax
 import jax.numpy as jnp
 from jax import lax
+from jax.experimental import pallas as pl
+from jax.experimental.pallas import tpu as pltpu
 from jax.sharding import PartitionSpec as P
 
 MOST = 2
-
+MESH = pl.DeviceIdType.MESH
+F32 = jnp.float32
+BF16 = jnp.bfloat16
 
 adapter_scale = 2.0
 
 
-def per_device(tokens, key_weight, down_proj, up_proj, tenant_of_row, page_of_tenant):
+def split3(value):
+    high = value.astype(BF16)
+    rest = value - high.astype(F32)
+    mid = rest.astype(BF16)
+    low = (rest - mid.astype(F32)).astype(BF16)
+    return high, mid, low
+
+
+def dot3(left, right):
+    high, mid, low = split3(left)
+    dot = functools.partial(jnp.dot, preferred_element_type=F32)
+    return dot(high, right) + (dot(mid, right) + dot(low, right))
+
+
+def iota(shape, dim):
+    return lax.broadcasted_iota(jnp.int32, shape, dim)
+
+
+def to_column(row):
+    n = row.shape[1]
+    eye = iota((n, n), 0) == iota((n, n), 1)
+    return jnp.sum(jnp.where(eye, row, 0), axis=1, keepdims=True)
+
+
+def kernel(
+    tok_hbm, w_hbm, down_hbm, up_hbm, tenant_ref, page_ref,
+    out_ref,
+    tok, packed, recv, wfull, down, up, place, mine, other, delta, back, base,
+    local_sem, w_send, w_recv, t_send, t_recv, x_send, x_recv,
+    p_send, p_recv, d_send, d_recv,
+):
+    g, r, c = lax.axis_index("groups"), lax.axis_index("replica"), lax.axis_index("tensor")
+    replicas = lax.axis_size("replica")
+    zs = replicas // 2
+    z, x = r // 2, r % 2
+    rows, half_d = tok.shape[1], tok.shape[2]
+    slots = packed.shape[0]
+    block = slots // replicas
+    depth = w_hbm.shape[0]
+    piece = depth // 2
+    per_half = half_d // piece
+
+    load_tok = pltpu.make_async_copy(tok_hbm, tok.at[c], local_sem.at[0])
+    load_w = pltpu.make_async_copy(w_hbm, wfull.at[pl.ds(r * depth, depth)], local_sem.at[1])
+    load_down = pltpu.make_async_copy(down_hbm, down, local_sem.at[2])
+    load_up = pltpu.make_async_copy(up_hbm, up, local_sem.at[3])
+    load_tok.start()
+    load_w.start()
+    load_down.start()
+    load_up.start()
+
+    barrier = pltpu.get_barrier_semaphore()
+    for k in range(1, replicas):
+        pl.semaphore_signal(barrier, inc=1, device_id=(g, (r + k) % replicas, c), device_id_type=MESH)
+    pl.semaphore_signal(barrier, inc=1, device_id=(g, r, 1 - c), device_id_type=MESH)
+    pl.semaphore_signal(barrier, inc=1, device_id=(1 - g, r, c), device_id_type=MESH)
+
+    tenants = page_ref.shape[1]
+    tenant = tenant_ref[...]
+    same = to_column(tenant) == tenant
+    earlier = iota((rows, rows), 0) < iota((rows, rows), 1)
+    rank = jnp.sum(jnp.where(same & earlier, 1, 0), axis=0, keepdims=True)
+    page_col = to_column(page_ref[...])
+    hit = iota((tenants, rows), 0) == tenant
+    page = jnp.sum(jnp.where(hit, page_col, 0), axis=0, keepdims=True)
+    slot = page * MOST + rank
+    place[...] = jnp.where(iota((slots, rows), 0) == slot, 1.0, 0.0).astype(BF16)
+    slot_col = to_column(slot)
+
+    load_tok.wait()
+    width = 512
+
+    def pack(j, _):
+        cols = pl.ds(pl.multiple_of(j * width, width), width)
+        packed[:, cols] = jnp.dot(
+            place[...], tok[c, :, cols], preferred_element_type=F32
+        ).astype(BF16)
+        return 0
+
+    lax.fori_loop(0, half_d // width, pack, 0)
+    load_w.wait()
+    pl.semaphore_wait(barrier, replicas + 1)
+
+    def w_rows(zz, xx, hh):
+        return pl.ds(pl.multiple_of(((zz * 2 + xx) * 2 + hh) * piece, piece), piece)
+
+    def w_copy(zz, xx, hh, way, device):
+        pid = (zz * 2 + xx) * 2 + hh
+        return pltpu.make_async_remote_copy(
+            src_ref=wfull.at[w_rows(zz, xx, hh)],
+            dst_ref=wfull.at[w_rows(zz, xx, hh)],
+            send_sem=w_send.at[way, pid],
+            recv_sem=w_recv.at[pid],
+            device_id=device,
+            device_id_type=MESH,
+        )
+
+    up_z = (g, jnp.minimum(r + 2, replicas - 1), c)
+    down_z = (g, jnp.maximum(r - 2, 0), c)
+    x_dev = (g, r + 1 - 2 * x, c)
+    y_dev = (1 - g, r, c)
+    core_dev = (g, r, 1 - c)
+
+    @pl.when(z < zs - 1)
+    def _():
+        w_copy(z, x, g, 0, up_z).start()
+
+    @pl.when(z > 0)
+    def _():
+        w_copy(z, x, g, 1, down_z).start()
+
+    w_copy(z, x, g, 2, x_dev).start()
+
+    tok_copy = pltpu.make_async_remote_copy(
+        src_ref=tok.at[c], dst_ref=tok.at[c], send_sem=x_send, recv_sem=x_recv,
+        device_id=core_dev, device_id_type=MESH,
+    )
+    tok_copy.start()
+
+    def block_rows(q):
+        return pl.ds(pl.multiple_of(q * block, block), block)
+
+    def t_copy(q):
+        return pltpu.make_async_remote_copy(
+            src_ref=packed.at[block_rows(q)], dst_ref=recv.at[block_rows(r)],
+            send_sem=t_send.at[q], recv_sem=t_recv.at[r],
+            device_id=(g, q, c), device_id_type=MESH,
+        )
+
+    def peer(d, e):
+        return ((z + d) % zs) * 2 + (x + e) % 2
+
+    for d in range(zs):
+        for e in range(2):
+            if d or e:
+                t_copy(peer(d, e)).start()
+    recv[block_rows(r)] = packed[block_rows(r)]
+
+    for d in range(1, zs):
+        @pl.when(z - d >= 0)
+        def _():
+            w_copy(z - d, x, g, 0, up_z).wait_recv()
+
+            @pl.when(z < zs - 1)
+            def _():
+                w_copy(z - d, x, g, 0, up_z).start()
+
+            w_copy(z - d, x, g, 2, x_dev).start()
+            w_copy(z - d, x, g, 3, y_dev).start()
+
+        @pl.when(z + d < zs)
+        def _():
+            w_copy(z + d, x, g, 1, down_z).wait_recv()
+
+            @pl.when(z > 0)
+            def _():
+                w_copy(z + d, x, g, 1, down_z).start()
+
+            w_copy(z + d, x, g, 2, x_dev).start()
+            w_copy(z + d, x, g, 3, y_dev).start()
+
+    for d in range(zs):
+        zz = (z + d) % zs
+        w_copy(zz, 1 - x, g, 2, x_dev).wait_recv()
+        w_copy(zz, 1 - x, g, 3, y_dev).start()
+
+    load_down.wait()
+    load_up.wait()
+    pair = 2 * block
+    rank_n = down.shape[0] // (block // MOST)
+    keep = (iota((pair, down.shape[0]), 0) % block) // MOST == iota((pair, down.shape[0]), 1) // rank_n
+
+    def pair_rows(zz):
+        return pl.ds(pl.multiple_of(zz * pair, pair), pair)
+
+    def p_copy(zz):
+        return pltpu.make_async_remote_copy(
+            src_ref=mine.at[pair_rows(zz)], dst_ref=other.at[pair_rows(zz)],
+            send_sem=p_send.at[zz], recv_sem=p_recv.at[zz],
+            device_id=core_dev, device_id_type=MESH,
+        )
+
+    def d_copy(q):
+        return pltpu.make_async_remote_copy(
+            src_ref=delta.at[block_rows(q)], dst_ref=back.at[block_rows(r)],
+            send_sem=d_send.at[q], recv_sem=d_recv.at[r],
+            device_id=(g, q, c), device_id_type=MESH,
+        )
+
+    def recv_wait(buffer, sems, q):
+        pltpu.make_async_remote_copy(
+            src_ref=buffer.at[block_rows(q)], dst_ref=buffer.at[block_rows(q)],
+            send_sem=sems.at[q], recv_sem=sems.at[q],
+            device_id=(g, q, c), device_id_type=MESH,
+        ).wait_recv()
+
+    def finish(d):
+        zz = (z + d) % zs
+        p_copy(zz).wait_recv()
+        shrink = mine[pair_rows(zz)] + other[pair_rows(zz)]
+        delta[pair_rows(zz)] = dot3(shrink, up[...])
+        for e in range(2):
+            if d or e:
+                d_copy(peer(d, e)).start()
+        if d == 0:
+            back[block_rows(r)] = delta[block_rows(r)]
+
+    for d in range(zs):
+        zz = (z + d) % zs
+        for e in range(2):
+            if d or e:
+                recv_wait(recv, t_recv, peer(d, e))
+        part = lax.dot_general(
+            recv[pair_rows(zz)], down[...], (((1,), (1,)), ((), ())), preferred_element_type=F32
+        )
+        mine[pair_rows(zz)] = jnp.where(keep, part, 0.0)
+        p_copy(zz).start()
+        if d:
+            finish(d - 1)
+    finish(zs - 1)
+
+    tok_copy.wait_recv()
+    for d in range(zs):
+        zz = (z + d) % zs
+        if d:
+            w_copy(zz, x, 1 - g, 3, y_dev).wait_recv()
+        w_copy(zz, 1 - x, 1 - g, 3, y_dev).wait_recv()
+    base[...] = jnp.zeros_like(base)
+
+    def add_piece(pid, _):
+        cols = pl.ds(pl.multiple_of((pid % per_half) * piece, piece), piece)
+        base[...] += jnp.dot(
+            tok[pid // per_half, :, cols],
+            wfull[pl.ds(pl.multiple_of(pid * piece, piece), piece)],
+            preferred_element_type=F32,
+        )
+        return 0
+
+    lax.fori_loop(0, 2 * per_half, add_piece, 0)
+
+    for d in range(zs):
+        for e in range(2):
+            if d or e:
+                recv_wait(back, d_recv, peer(d, e))
+    spread = jnp.where(iota((rows, slots), 1) == slot_col, 1.0, 0.0).astype(BF16)
+    dot = functools.partial(jnp.dot, preferred_element_type=F32)
+    high, mid, low = split3(back[...])
+    per_row = dot(spread, high) + (dot(spread, mid) + dot(spread, low))
+    out_ref[...] = (base[...] + adapter_scale * per_row).astype(out_ref.dtype)
+
+    tok_copy.wait_send()
+
+    @pl.when(z < zs - 1)
+    def _():
+        w_copy(z, x, g, 0, up_z).wait_send()
+
+    @pl.when(z > 0)
+    def _():
+        w_copy(z, x, g, 1, down_z).wait_send()
+
+    w_copy(z, x, g, 2, x_dev).wait_send()
+    for d in range(1, zs):
+        @pl.when(z - d >= 0)
+        def _():
+            @pl.when(z < zs - 1)
+            def _():
+                w_copy(z - d, x, g, 0, up_z).wait_send()
+
+            w_copy(z - d, x, g, 2, x_dev).wait_send()
+            w_copy(z - d, x, g, 3, y_dev).wait_send()
+
+        @pl.when(z + d < zs)
+        def _():
+            @pl.when(z > 0)
+            def _():
+                w_copy(z + d, x, g, 1, down_z).wait_send()
+
+            w_copy(z + d, x, g, 2, x_dev).wait_send()
+            w_copy(z + d, x, g, 3, y_dev).wait_send()
+
+    for d in range(zs):
+        zz = (z + d) % zs
+        w_copy(zz, 1 - x, g, 3, y_dev).wait_send()
+        p_copy(zz).wait_send()
+        for e in range(2):
+            if d or e:
+                t_copy(peer(d, e)).wait_send()
+                d_copy(peer(d, e)).wait_send()
+
+
+def fused(tokens, key_weight, down_proj, up_proj, tenant_of_row, page_of_tenant):
+    rows, half_d = tokens.shape
+    depth, cols = key_weight.shape
+    ten_dev, rank_n, _ = down_proj.shape
+    replicas = lax.axis_size("replica")
+    slots = replicas * ten_dev * MOST
+    feats = ten_dev * rank_n
+    any_space = pl.BlockSpec(memory_space=pl.ANY)
+    vmem = pl.BlockSpec(memory_space=pltpu.VMEM)
+    dma = pltpu.SemaphoreType.DMA
+    return pl.pallas_call(
+        kernel,
+        out_shape=jax.ShapeDtypeStruct((rows, cols), BF16),
+        in_specs=[any_space] * 4 + [vmem] * 2,
+        out_specs=vmem,
+        scratch_shapes=[
+            pltpu.VMEM((2, rows, half_d), BF16),
+            pltpu.VMEM((slots, half_d), BF16),
+            pltpu.VMEM((slots, half_d), BF16),
+            pltpu.VMEM((replicas * depth, cols), BF16),
+            pltpu.VMEM((feats, half_d), BF16),
+            pltpu.VMEM((feats, cols), BF16),
+            pltpu.VMEM((slots, rows), BF16),
+            pltpu.VMEM((slots, feats), F32),
+            pltpu.VMEM((slots, feats), F32),
+            pltpu.VMEM((slots, cols), F32),
+            pltpu.VMEM((slots, cols), F32),
+            pltpu.VMEM((rows, cols), F32),
+            dma((4,)),
+            dma((4, 2 * replicas)),
+            dma((2 * replicas,)),
+            dma((replicas,)),
+            dma((replicas,)),
+            dma,
+            dma,
+            dma((replicas // 2,)),
+            dma((replicas // 2,)),
+            dma((replicas,)),
+            dma((replicas,)),
+        ],
+        compiler_params=pltpu.CompilerParams(
+            collective_id=0, has_side_effects=True, vmem_limit_bytes=40 * 2**20
+        ),
+        cost_estimate=pl.CostEstimate(
+            flops=2 * rows * 2 * half_d * cols + 4 * slots * half_d * feats,
+            bytes_accessed=2 * (rows * half_d + depth * cols + feats * half_d),
+            transcendentals=0,
+        ),
+        name="adapted_key",
+    )(
+        tokens,
+        key_weight,
+        down_proj.reshape(feats, half_d),
+        up_proj.reshape(feats, cols),
+        tenant_of_row.reshape(1, rows),
+        page_of_tenant.reshape(1, -1),
+    )
+
+
+def plain(tokens, key_weight, down_proj, up_proj, tenant_of_row, page_of_tenant):
     row_count = tokens.shape[0]
     ten_dev = down_proj.shape[0]
     replicas = lax.axis_size("replica")
@@ -47,6 +402,20 @@
     return (base_total_sum + adapter_scale * per_row_delta).astype(jnp.bfloat16)
 
 
+def per_device(tokens, key_weight, down_proj, up_proj, tenant_of_row, page_of_tenant):
+    args = (tokens, key_weight, down_proj, up_proj, tenant_of_row, page_of_tenant)
+    replicas = lax.axis_size("replica")
+    tiles = (
+        lax.axis_size("groups") == 2
+        and lax.axis_size("tensor") == 2
+        and replicas % 2 == 0
+        and (down_proj.shape[0] * MOST) % 16 == 0
+        and key_weight.shape[0] % 256 == 0
+        and tokens.shape[1] % 512 == 0
+    )
+    return fused(*args) if tiles else plain(*args)
+
+
 def solution(mesh):
     return jax.shard_map(
         per_device,

time: 162 us -> 111 us (0.69)
  Pallas kernels: 0 us -> 104 us
  blocking collectives: 102 us -> 0 us
  between operations: 13.5 us -> 0.02 us
  local copies, waits for them, and re-layouts: 20.1 us -> 7.12 us
  waiting for transfers between devices: 11.1 us -> 0 us
  matrix products: 7.12 us -> 0 us
  other arithmetic: 3.95 us -> 0 us
  starting transfers between devices: 3.45 us -> 0 us
    pallas_call x0 -> x1, Pallas kernels: none -> 104 us  [fused(): pl.pallas_call(kernel, out_shape=jax.ShapeDtypeStruct((rows, cols), BF16)...]
    all_to_all x1 -> x0, blocking collectives: 98.1 us -> none  [per_device(): lax.all_to_all(packed, 'replica', split_axis=0, concat_axis=0, tiled=True)]
    gather x4 -> x0, local copies, waits for them, and re-layouts: 14.5 us -> none  [the longest x2 11.7 us: per_device(): jnp.take(padded, slot_source, axis=0)]
    all_to_all x1 -> x0, waiting for transfers between devices: 9.61 us -> none  [per_device(): lax.all_to_all(adapter_delta_rows, 'replica', split_axis=0, concat_axis=0...]
    dot_general x3 -> x0, matrix products: 7.12 us -> none  [the longest x1 5.38 us: per_device(): jnp.dot(gathered, lax.all_gather(key_weight, 'replica', axis=0, tiled=Tru...]
    unnamed x8 -> x13, local copies, waits for them, and re-layouts: 0.02 us -> 7.12 us
    psum x1 -> x0, blocking collectives: 3.74 us -> none  [per_device(): shrink = lax.psum(partial_value, 'tensor')]
    select_n x4 -> x0, other arithmetic: 3.72 us -> none  [the longest x2 3.7 us: per_device(): jnp.take(padded, slot_source, axis=0)]
  transfers between devices with their start and end apart: 3 -> 0, of which waited for: 1 -> 0; matrix products, arithmetic and copies ran while one was open for 16% -> 0% of each run, Pallas kernels for 0% -> 0%
where the time goes in v1:
time: 111 us
  Pallas kernels  104 us (94%)
  local copies, waits for them, and re-layouts  7.12 us (6%)
    pallas_call x1, Pallas kernels, fused(): pl.pallas_call(kernel, out_shape=jax.ShapeDtypeStruct((rows, cols), BF16)...  104 us
    unnamed x13, local copies, waits for them, and re-layouts  7.12 us

profile of v1, /device:TPU:0, one launch (start us, length us, event | category | flops | bytes accessed | tf_op | source)
XLA Modules:
  0.0 111.2 jit_solution(7413800503488450917)
XLA Ops:
  0.0 0.0 copy-start
  0.0 1.6 %copy-done = bf16[256,4096]{1,0:T(8,128)(2,1)S(1)} copy-done((bf16[256,4096]{1,0:T(8,128)(2,1)S(1)}, bf16[256,4096]{1,0:T(8,128)(2,1)}, u32[]{:S(2)}) %copy-start) | copy-done | bytes 2097176
  1.6 0.0 copy-start.1
  1.6 1.6 %copy-done.1 = bf16[16,16,4096]{2,1,0:T(8,128)(2,1)S(1)} copy-done((bf16[16,16,4096]{2,1,0:T(8,128)(2,1)S(1)}, bf16[16,16,4096]{2,1,0:T(8,128)(2,1)}, u32[]{:S(2)}) %copy-start.1) | copy-done | bytes 2097176
  3.2 0.0 copy-start.2
  3.2 1.0 copy-done.2
  4.2 0.0 copy-start.3
  4.2 0.9 copy-done.3
  5.1 0.0 copy-start.4
  5.1 0.7 copy-done.4
  5.8 0.0 copy-start.5
  5.8 0.7 copy-done.5
  6.5 104.1 %adapted_key.1 = bf16[256,256]{1,0:T(8,128)(2,1)S(1)} custom-call(bf16[256,4096]{1,0:T(8,128)(2,1)S(1)} %copy-done, bf16[1024,256]{1,0:T(8,128)(2,1)S(1)} %copy-done.2, bf16[256,4096]{1,0:T(8,128)(2,1)S(1)} %bitcast.4, bf16[256,256]{1,0:T(8,128)(2,1)S(1)} %bitcast.5, s32[1,256]{1,0:T(1,128)S(1)} %bitcast.6, s32[1,128]{1,0:T(1,128)S(1)} %bitcast.7), custom_call_target="tpu_custom_call" | custom-call | flops 2147483648 | bytes 4718592 | tf_op jit(solution)/shard_map/adapted_key/pallas_call | solution.py:318
  110.6 0.7 copy.8
Async XLA Ops:
  0.0 1.6 %copy-start = (bf16[256,4096]{1,0:T(8,128)(2,1)S(1)}, bf16[256,4096]{1,0:T(8,128)(2,1)}, u32[]{:S(2)}) copy-start(bf16[256,4096]{1,0:T(8,128)(2,1)} %tok_hbm.1) | copy-start | bytes 6291460
  1.6 1.6 %copy-start.1 = (bf16[16,16,4096]{2,1,0:T(8,128)(2,1)S(1)}, bf16[16,16,4096]{2,1,0:T(8,128)(2,1)}, u32[]{:S(2)}) copy-start(bf16[16,16,4096]{2,1,0:T(8,128)(2,1)} %param.8) | copy-start | bytes 6291460
  3.2 1.0 copy-start.2
  4.2 0.9 copy-start.3
  5.1 0.7 copy-start.4
  5.8 0.7 copy-start.5

commit v2 on v1

--- a/solution.py
+++ b/solution.py
@@ -147,13 +147,9 @@
     def peer(d, e):
         return ((z + d) % zs) * 2 + (x + e) % 2
 
-    for d in range(zs):
-        for e in range(2):
-            if d or e:
-                t_copy(peer(d, e)).start()
     recv[block_rows(r)] = packed[block_rows(r)]
 
-    for d in range(1, zs):
+    def pass_z(d):
         @pl.when(z - d >= 0)
         def _():
             w_copy(z - d, x, g, 0, up_z).wait_recv()
@@ -176,10 +172,30 @@
             w_copy(z + d, x, g, 2, x_dev).start()
             w_copy(z + d, x, g, 3, y_dev).start()
 
-    for d in range(zs):
+    def pass_x(d):
         zz = (z + d) % zs
         w_copy(zz, 1 - x, g, 2, x_dev).wait_recv()
         w_copy(zz, 1 - x, g, 3, y_dev).start()
+
+    def send_rows(*steps):
+        for step in steps:
+            for e in range(2):
+                t_copy(peer(step, e)).start()
+
+    t_copy(peer(0, 1)).start()
+    far = [d for d in range(2, zs)] + ([1] if zs > 1 else [])
+    for d in range(1, min(3, zs)):
+        pass_z(d)
+    send_rows(*far[:1])
+    for d in range(3, zs):
+        pass_z(d)
+    pass_x(0)
+    send_rows(*far[1:2])
+    for d in range(1, min(2, zs)):
+        pass_x(d)
+    send_rows(*far[2:])
+    for d in range(2, zs):
+        pass_x(d)
 
     load_down.wait()
     load_up.wait()
@@ -346,7 +362,7 @@
             dma((replicas,)),
         ],
         compiler_params=pltpu.CompilerParams(
-            collective_id=0, has_side_effects=True, vmem_limit_bytes=40 * 2**20
+            collective_id=0, has_side_effects=True, vmem_limit_bytes=60 * 2**20
         ),
         cost_estimate=pl.CostEstimate(
             flops=2 * rows * 2 * half_d * cols + 4 * slots * half_d * feats,

time: 111 us -> 83.1 us (0.75)
  Pallas kernels: 104 us -> 81.3 us
  local copies, waits for them, and re-layouts: 7.12 us -> 1.57 us
    pallas_call x1, Pallas kernels: 104 us -> 81.3 us  [fused(): pl.pallas_call(kernel, out_shape=jax.ShapeDtypeStruct((rows, cols), BF16)...]
    unnamed x13 -> x1, local copies, waits for them, and re-layouts: 7.12 us -> 1.57 us
where the time goes in v2:
time: 83.1 us; the launch traced here: 82.9 us
  Pallas kernels  81.3 us (98%)
  local copies, waits for them, and re-layouts  1.57 us (2%)
    pallas_call x1, Pallas kernels, fused(): pl.pallas_call(kernel, out_shape=jax.ShapeDtypeStruct((rows, cols), BF16)...  81.3 us

profile of v2, /device:TPU:0, one launch (start us, length us, event | category | flops | bytes accessed | tf_op | source)
XLA Modules:
  0.0 82.9 jit_solution(13653752197197588304)
XLA Ops:
  0.0 81.3 %adapted_key.1 = bf16[256,256]{1,0:T(8,128)(2,1)} custom-call(bf16[256,4096]{1,0:T(8,128)(2,1)} %tok_hbm.1, bf16[1024,256]{1,0:T(8,128)(2,1)} %w_hbm.1, bf16[256,4096]{1,0:T(8,128)(2,1)} %bitcast.4, bf16[256,256]{1,0:T(8,128)(2,1)} %bitcast.5, s32[1,256]{1,0:T(1,128)} %bitcast.6, s32[1,128]{1,0:T(1,128)} %bitcast.7), custom_call_target="tpu_custom_call" | custom-call | flops 2147483648 | bytes 4718592 | tf_op jit(solution)/shard_map/adapted_key/pallas_call | solution.py:334
  81.3 1.6 %copy.8 = bf16[256,256]{1,0:T(8,128)(2,1)} copy(bf16[256,256]{1,0:T(8,128)(2,1)} %adapted_key.1) | data formatting | bytes 262144

commit v3 on v1

--- a/solution.py
+++ b/solution.py
@@ -61,8 +61,8 @@
     load_w = pltpu.make_async_copy(w_hbm, wfull.at[pl.ds(r * depth, depth)], local_sem.at[1])
     load_down = pltpu.make_async_copy(down_hbm, down, local_sem.at[2])
     load_up = pltpu.make_async_copy(up_hbm, up, local_sem.at[3])
+    load_w.start()
     load_tok.start()
-    load_w.start()
     load_down.start()
     load_up.start()
 
@@ -71,6 +71,39 @@
         pl.semaphore_signal(barrier, inc=1, device_id=(g, (r + k) % replicas, c), device_id_type=MESH)
     pl.semaphore_signal(barrier, inc=1, device_id=(g, r, 1 - c), device_id_type=MESH)
     pl.semaphore_signal(barrier, inc=1, device_id=(1 - g, r, c), device_id_type=MESH)
+
+    load_w.wait()
+    pl.semaphore_wait(barrier, replicas + 1)
+
+    def w_rows(zz, xx, hh):
+        return pl.ds(pl.multiple_of(((zz * 2 + xx) * 2 + hh) * piece, piece), piece)
+
+    def w_copy(zz, xx, hh, way, device):
+        pid = (zz * 2 + xx) * 2 + hh
+        return pltpu.make_async_remote_copy(
+            src_ref=wfull.at[w_rows(zz, xx, hh)],
+            dst_ref=wfull.at[w_rows(zz, xx, hh)],
+            send_sem=w_send.at[way, pid],
+            recv_sem=w_recv.at[pid],
+            device_id=device,
+            device_id_type=MESH,
+        )
+
+    up_z = (g, jnp.minimum(r + 2, replicas - 1), c)
+    down_z = (g, jnp.maximum(r - 2, 0), c)
+    x_dev = (g, r + 1 - 2 * x, c)
+    y_dev = (1 - g, r, c)
+    core_dev = (g, r, 1 - c)
+
+    @pl.when(z < zs - 1)
+    def _():
+        w_copy(z, x, g, 0, up_z).start()
+
+    @pl.when(z > 0)
+    def _():
+        w_copy(z, x, g, 1, down_z).start()
+
+    w_copy(z, x, g, 2, x_dev).start()
 
     tenants = page_ref.shape[1]
     tenant = tenant_ref[...]
@@ -85,6 +118,11 @@
     slot_col = to_column(slot)
 
     load_tok.wait()
+    tok_copy = pltpu.make_async_remote_copy(
+        src_ref=tok.at[c], dst_ref=tok.at[c], send_sem=x_send, recv_sem=x_recv,
+        device_id=core_dev, device_id_type=MESH,
+    )
+    tok_copy.start()
     width = 512
 
     def pack(j, _):
@@ -95,45 +133,6 @@
         return 0
 
     lax.fori_loop(0, half_d // width, pack, 0)
-    load_w.wait()
-    pl.semaphore_wait(barrier, replicas + 1)
-
-    def w_rows(zz, xx, hh):
-        return pl.ds(pl.multiple_of(((zz * 2 + xx) * 2 + hh) * piece, piece), piece)
-
-    def w_copy(zz, xx, hh, way, device):
-        pid = (zz * 2 + xx) * 2 + hh
-        return pltpu.make_async_remote_copy(
-            src_ref=wfull.at[w_rows(zz, xx, hh)],
-            dst_ref=wfull.at[w_rows(zz, xx, hh)],
-            send_sem=w_send.at[way, pid],
-            recv_sem=w_recv.at[pid],
-            device_id=device,
-            device_id_type=MESH,
-        )
-
-    up_z = (g, jnp.minimum(r + 2, replicas - 1), c)
-    down_z = (g, jnp.maximum(r - 2, 0), c)
-    x_dev = (g, r + 1 - 2 * x, c)
-    y_dev = (1 - g, r, c)
-    core_dev = (g, r, 1 - c)
-
-    @pl.when(z < zs - 1)
-    def _():
-        w_copy(z, x, g, 0, up_z).start()
-
-    @pl.when(z > 0)
-    def _():
-        w_copy(z, x, g, 1, down_z).start()
-
-    w_copy(z, x, g, 2, x_dev).start()
-
-    tok_copy = pltpu.make_async_remote_copy(
-        src_ref=tok.at[c], dst_ref=tok.at[c], send_sem=x_send, recv_sem=x_recv,
-        device_id=core_dev, device_id_type=MESH,
-    )
-    tok_copy.start()
-
     def block_rows(q):
         return pl.ds(pl.multiple_of(q * block, block), block)
 
@@ -144,16 +143,21 @@
             device_id=(g, q, c), device_id_type=MESH,
         )
 
+    def mirror(d):
+        zz = z
+        bit = 1
+        while bit < zs:
+            if d & bit:
+                zz = zz + bit - 2 * bit * ((zz // bit) % 2)
+            bit *= 2
+        return zz
+
     def peer(d, e):
-        return ((z + d) % zs) * 2 + (x + e) % 2
-
-    for d in range(zs):
-        for e in range(2):
-            if d or e:
-                t_copy(peer(d, e)).start()
+        return mirror(d) * 2 + (x + e) % 2
+
     recv[block_rows(r)] = packed[block_rows(r)]
 
-    for d in range(1, zs):
+    def pass_z(d):
         @pl.when(z - d >= 0)
         def _():
             w_copy(z - d, x, g, 0, up_z).wait_recv()
@@ -176,10 +180,27 @@
             w_copy(z + d, x, g, 2, x_dev).start()
             w_copy(z + d, x, g, 3, y_dev).start()
 
-    for d in range(zs):
-        zz = (z + d) % zs
-        w_copy(zz, 1 - x, g, 2, x_dev).wait_recv()
-        w_copy(zz, 1 - x, g, 3, y_dev).start()
+    def pass_x(d):
+        for step in sorted({-d, d}):
+            @pl.when((z + step >= 0) & (z + step < zs))
+            def _():
+                w_copy(z + step, 1 - x, g, 2, x_dev).wait_recv()
+                w_copy(z + step, 1 - x, g, 3, y_dev).start()
+
+    t_copy(peer(0, 1)).start()
+    pass_z(1)
+    pass_z(2)
+    t_copy(peer(3, 1)).start()
+    t_copy(peer(3, 0)).start()
+    pass_z(3)
+    pass_x(0)
+    t_copy(peer(2, 1)).start()
+    t_copy(peer(2, 0)).start()
+    pass_x(1)
+    t_copy(peer(1, 1)).start()
+    t_copy(peer(1, 0)).start()
+    pass_x(2)
+    pass_x(3)
 
     load_down.wait()
     load_up.wait()
@@ -212,7 +233,7 @@
         ).wait_recv()
 
     def finish(d):
-        zz = (z + d) % zs
+        zz = mirror(d)
         p_copy(zz).wait_recv()
         shrink = mine[pair_rows(zz)] + other[pair_rows(zz)]
         delta[pair_rows(zz)] = dot3(shrink, up[...])
@@ -222,8 +243,8 @@
         if d == 0:
             back[block_rows(r)] = delta[block_rows(r)]
 
-    for d in range(zs):
-        zz = (z + d) % zs
+    def adapter(d):
+        zz = mirror(d)
         for e in range(2):
             if d or e:
                 recv_wait(recv, t_recv, peer(d, e))
@@ -232,28 +253,44 @@
         )
         mine[pair_rows(zz)] = jnp.where(keep, part, 0.0)
         p_copy(zz).start()
-        if d:
-            finish(d - 1)
-    finish(zs - 1)
+
+    order = [0, 3, 2, 1]
+    for i, d in enumerate(order[:-1]):
+        adapter(d)
+        if i:
+            finish(order[i - 1])
+    finish(order[-2])
+
+    def add_piece(zz, xx, hh):
+        pid = (zz * 2 + xx) * 2 + hh
+        cols = pl.ds(pl.multiple_of((pid % per_half) * piece, piece), piece)
+        base[...] += jnp.dot(
+            tok[pid // per_half, :, cols],
+            wfull[w_rows(zz, xx, hh)],
+            preferred_element_type=F32,
+        )
 
     tok_copy.wait_recv()
+    base[...] = jnp.zeros_like(base)
+
+    def add_near(zz, _):
+        add_piece(zz, x, g)
+        add_piece(zz, 1 - x, g)
+        return 0
+
+    lax.fori_loop(0, zs, add_near, 0)
+    add_piece(z, x, 1 - g)
+
+    adapter(order[-1])
+    finish(order[-1])
+
     for d in range(zs):
         zz = (z + d) % zs
         if d:
             w_copy(zz, x, 1 - g, 3, y_dev).wait_recv()
+            add_piece(zz, x, 1 - g)
         w_copy(zz, 1 - x, 1 - g, 3, y_dev).wait_recv()
-    base[...] = jnp.zeros_like(base)
-
-    def add_piece(pid, _):
-        cols = pl.ds(pl.multiple_of((pid % per_half) * piece, piece), piece)
-        base[...] += jnp.dot(
-            tok[pid // per_half, :, cols],
-            wfull[pl.ds(pl.multiple_of(pid * piece, piece), piece)],
-            preferred_element_type=F32,
-        )
-        return 0
-
-    lax.fori_loop(0, 2 * per_half, add_piece, 0)
+        add_piece(zz, 1 - x, 1 - g)
 
     for d in range(zs):
         for e in range(2):
@@ -346,7 +383,7 @@
             dma((replicas,)),
         ],
         compiler_params=pltpu.CompilerParams(
-            collective_id=0, has_side_effects=True, vmem_limit_bytes=40 * 2**20
+            collective_id=0, has_side_effects=True, vmem_limit_bytes=60 * 2**20
         ),
         cost_estimate=pl.CostEstimate(
             flops=2 * rows * 2 * half_d * cols + 4 * slots * half_d * feats,
@@ -408,7 +445,7 @@
     tiles = (
         lax.axis_size("groups") == 2
         and lax.axis_size("tensor") == 2
-        and replicas % 2 == 0
+        and replicas == 8
         and (down_proj.shape[0] * MOST) % 16 == 0
         and key_weight.shape[0] % 256 == 0
         and tokens.shape[1] % 512 == 0

time: 111 us -> 77.5 us (0.70)
  Pallas kernels: 104 us -> 75.8 us
  local copies, waits for them, and re-layouts: 7.12 us -> 1.57 us
    pallas_call x1, Pallas kernels: 104 us -> 75.8 us  [fused(): pl.pallas_call(kernel, out_shape=jax.ShapeDtypeStruct((rows, cols), BF16)...]
    unnamed x13 -> x1, local copies, waits for them, and re-layouts: 7.12 us -> 1.57 us
where the time goes in v3:
time: 77.5 us; the launch traced here: 77.4 us
  Pallas kernels  75.8 us (98%)
  local copies, waits for them, and re-layouts  1.57 us (2%)
    pallas_call x1, Pallas kernels, fused(): pl.pallas_call(kernel, out_shape=jax.ShapeDtypeStruct((rows, cols), BF16)...  75.8 us
    unnamed x1, local copies, waits for them, and re-layouts  1.57 us

profile of v3, /device:TPU:0, one launch (start us, length us, event | category | flops | bytes accessed | tf_op | source)
XLA Modules:
  0.0 77.4 jit_solution(17323847618645655613)
XLA Ops:
  0.0 75.8 %adapted_key.1 = bf16[256,256]{1,0:T(8,128)(2,1)} custom-call(bf16[256,4096]{1,0:T(8,128)(2,1)} %tok_hbm.1, bf16[1024,256]{1,0:T(8,128)(2,1)} %w_hbm.1, bf16[256,4096]{1,0:T(8,128)(2,1)} %bitcast.4, bf16[256,256]{1,0:T(8,128)(2,1)} %bitcast.5, s32[1,256]{1,0:T(1,128)} %bitcast.6, s32[1,128]{1,0:T(1,128)} %bitcast.7), custom_call_target="tpu_custom_call" | custom-call | flops 2147483648 | bytes 4718592 | tf_op jit(solution)/shard_map/adapted_key/pallas_call | solution.py:355
  75.8 1.6 %copy.8 = bf16[256,256]{1,0:T(8,128)(2,1)} copy(bf16[256,256]{1,0:T(8,128)(2,1)} %adapted_key.1) | data formatting | bytes 262144
